TPU v7x, 512 devices: a whole 4x4x16 slice. The times are simulated.
512 devices in a mesh: row: 16 (over x, y_hi, core), col: 32 (over y_lo, z).
Axes of the slice: x: 4, y: 4 (y_hi: 2, y_lo: 2; y = y_hi * 2 + y_lo), z: 16, core: 2. Of those that a mesh axis runs over, the one named last changes fastest.
Arguments:
- rhs: bfloat16 [49152, 8192], P('row', 'col'), may hold values from -6 to 6
- panel_columns: bfloat16 [2, 256, 49152], P(None, 'col', 'row'), may hold values from -0.375 to 0.375
- diag_inverse: float32 [2, 256, 256], replicated, may hold values from -2 to 2, as said below
- block_order: int32 [192], replicated, may hold values from 0 to 191, each once
Outputs:
- solved_rhs: bfloat16 [49152, 8192], P('row', 'col')
- gram: float32 [8192, 8192], P('row', 'col')
Inputs may be any that keep to these rules, and one draw needn't show every extreme that they name: `diag_inverse`: each of the two matrices is lower triangular with a diagonal between 0.4 and 2.
All inputs are finite; a program needn't handle non-finite values.
Results may differ from a plain program's by a relative error of at most 0.0059.
Values may be sent and summed in bfloat16 or wider, within the bound.
A program may use at most 64 MiB of HBM per device.

v0:
```python
import jax
import jax.numpy as jnp
from jax import lax
from jax.sharding import PartitionSpec as P


def broadcast(value, axis, source):
    kept = jnp.where(lax.axis_index(axis) == source, value, 0).astype(value.dtype)
    return lax.psum(kept, axis)


def contract_rows(factor, solved):
    return lax.dot_general(
        factor, solved, (((0,), (0,)), ((), ())), preferred_element_type=jnp.float32
    )


def shards(rhs, panel_columns, diag_inverse, block_order):
    block = diag_inverse.shape[1]
    rows = rhs.shape[0]
    nblocks = rows // block
    width = rhs.shape[1]
    row_index = lax.axis_index("row")
    local_ids = row_index * nblocks + jnp.arange(nblocks, dtype=jnp.int32)
    first = jnp.argmax(block_order == 0)
    second = jnp.argmax(block_order == 1)

    def slice_block(work, position):
        return lax.dynamic_slice_in_dim(work, position % nblocks * block, block, 0)

    def solve_block(target, step, position):
        product = jnp.dot(
            diag_inverse[step],
            target.astype(jnp.float32),
            precision=lax.Precision.HIGHEST,
            preferred_element_type=jnp.float32,
        )
        return broadcast(product.astype(jnp.bfloat16), "row", position // nblocks)

    def panel_update(work, step, solved, active):
        whole_panel = lax.all_gather(panel_columns[step], "col", axis=0, tiled=True)
        change = contract_rows(whole_panel, solved)
        fresh = (
            (work.astype(jnp.float32) - change).astype(jnp.bfloat16).reshape(nblocks, block, width)
        )
        blocks = work.reshape(nblocks, block, width)
        return jnp.where(active[:, None, None], fresh, blocks).reshape(rows, width)

    def place(work, solved, position):
        blocks = work.reshape(nblocks, block, width)
        hit = (local_ids == position)[:, None, None]
        return jnp.where(hit, solved[None], blocks).reshape(rows, width)

    first_block = solve_block(slice_block(rhs, first), 0, first)
    work = panel_update(rhs, 0, first_block, local_ids != first)
    work = place(work, first_block, first)
    second_block = solve_block(slice_block(work, second), 1, second)
    work = panel_update(work, 1, second_block, (local_ids != first) & (local_ids != second))
    work = place(work, second_block, second)
    finished = jnp.concatenate([first_block, second_block], 0)
    span = width * lax.axis_size("col") // lax.axis_size("row")
    everything = lax.all_gather(finished, "col", axis=1, tiled=True)
    chosen = lax.dynamic_slice_in_dim(everything, row_index * span, span, 1)
    gram = lax.dot_general(
        chosen, finished, (((0,), (0,)), ((), ())), preferred_element_type=jnp.float32
    ) / (2 * block)
    return (work, gram)


def solution(mesh):
    in_specs = (P("row", "col"), P(None, "col", "row"), P(), P())
    out_specs = (P("row", "col"), P("row", "col"))
    return jax.shard_map(shards, mesh=mesh, in_specs=in_specs, out_specs=out_specs, check_vma=False)
```

profile of v0, /device:TPU:6, one launch (start us, length us, event | category | flops | bytes accessed | tf_op | source)
XLA Modules:
  0.0 493.1 jit_solution(6584796631347167590)
XLA Ops:
  8.0 1.4 compare_reduce_fusion
  11.3 2.0 fusion.11
  13.3 0.0 all-gather.8.cloned.1.call-start
  13.3 1.5 fusion.27
  14.8 0.0 all-reduce.5.cloned.1.call-start
  14.9 1.7 copy.10
  16.6 0.7 compare_reduce_fusion.1
  19.2 0.6 fusion.24
  19.8 0.1 broadcast_in_dim.79
  19.9 0.1 broadcast_in_dim.73
  20.0 143.8 %all-reduce.3.cloned.1.call-done = bf16[256,256]{0,1:T(8,128)(2,1)} async-done(((bf16[256,256]{0,1:T(8,128)(2,1)}), bf16[256,256]{0,1:T(8,128)(2,1)}) %all-reduce.3.cloned.1.call-update) | async-done | bytes 131088 | tf_op jit(solution)/shard_map/psum | solution.py:9
  163.8 1.0 copy.9
  164.8 0.1 broadcast_in_dim.77
  164.9 1.7 copy.12
  166.7 2.8 fusion.7
  169.5 1.1 copy-done.5
  170.6 1.0 fusion.13
  171.7 0.0 all-gather.10.cloned.1.call-start
  171.7 0.5 all-gather.10.cloned.1.call-update
  172.3 152.8 %all-reduce.5.cloned.1.call-done = bf16[256,256]{0,1:T(8,128)(2,1)} async-done(((bf16[256,256]{0,1:T(8,128)(2,1)}), bf16[256,256]{0,1:T(8,128)(2,1)}) %all-reduce.5.cloned.1.call-update) | async-done | bytes 131088 | tf_op jit(solution)/shard_map/psum | solution.py:9
  325.1 0.9 constant_dynamic-update-slice_fusion
  326.0 0.7 copy-done
  326.7 1.2 compare_and_fusion
  328.0 0.1 broadcast_in_dim.84
  328.0 0.1 broadcast_in_dim.70
  328.1 1.0 copy.13
  329.1 0.1 broadcast_in_dim.82
  329.3 0.9 copy.14
  330.2 4.5 fusion.6
  334.7 2.6 copy.15
  337.3 146.1 %all-gather.6.cloned.1.call-done = bf16[512,8192]{0,1:T(8,128)(2,1)} async-done(((bf16[512,256]{0,1:T(8,128)(2,1)}), bf16[512,8192]{0,1:T(8,128)(2,1)}) %all-gather.6.cloned.1.call-update) | async-done | bytes 8388624 | tf_op jit(solution)/shard_map/all_gather | solution.py:62
  483.4 2.2 convolution_multiply_fusion
  (25 shorter events, 0.3 us)
Async XLA Ops:
  8.0 155.8 %all-reduce.3.cloned.1.call-start = ((), (), s32[]{:S(2)}) async-start(), calls=%async_computation | async-start | bytes 262144 | tf_op jit(solution)/shard_map/psum | solution.py:9
  13.3 153.4 %all-gather.8.cloned.1.call-start = ((), (), s32[]{:S(2)}) async-start(), calls=%async_computation.3 | async-start | bytes 1622016 | tf_op jit(solution)/shard_map/all_gather | solution.py:41
  14.8 1.8 copy-start.6
  14.8 310.2 %all-reduce.5.cloned.1.call-start = ((), (), s32[]{:S(2)}) async-start(), calls=%async_computation.1 | async-start | bytes 262144 | tf_op jit(solution)/shard_map/psum | solution.py:9
  164.9 1.8 copy-start.3
  166.6 4.0 copy-start.2
  169.5 1.1 copy-start.5
  171.7 158.5 %all-gather.10.cloned.1.call-start = ((), (), s32[]{:S(2)}) async-start(), calls=%async_computation.4 | async-start | bytes 1622016 | tf_op jit(solution)/shard_map/all_gather | solution.py:41
  172.2 311.1 %all-gather.6.cloned.1.call-start = ((), (), s32[]{:S(2)}) async-start(), calls=%async_computation.2 | async-start | bytes 8650752 | tf_op jit(solution)/shard_map/all_gather | solution.py:62
  326.0 0.7 copy-start
  329.3 0.9 copy-start.4
  334.7 148.7 %copy-start.1 = (bf16[512,256]{0,1:T(8,128)(2,1)S(1)}, bf16[512,256]{0,1:T(8,128)(2,1)}, u32[]{:S(2)}) copy-start(bf16[512,256]{0,1:T(8,128)(2,1)} %copy-done) | copy-start | bytes 786436
Sparse Core Ops, SparseCore 0:
  13.4 150.2 all-reduce.2
  171.8 153.2 all-reduce.4
Sparse Core Ops, SparseCore 1:
  16.0 138.0 all-gather.7
  174.2 140.8 all-gather.9
  326.8 156.5 all-gather.5
where the time goes:
time: 494 us; the launch traced here: 493 us
  waiting for transfers between devices  443 us (90%)
  between operations  19.6 us (4%)
  local copies, waits for them, and re-layouts  13.8 us (3%)
  matrix products  12.5 us (3%)
    psum x2, waiting for transfers between devices, broadcast(): return lax.psum(kept, axis)  297 us
    all_gather x1, waiting for transfers between devices, shards(): everything = lax.all_gather(finished, 'col', axis=1, tiled=True)  146 us
  transfers between devices with their start and end apart: 5, of which 3 were waited for; matrix products, arithmetic and copies ran while one was open for 4% of the time, Pallas kernels for 0%

commit v1 on v0

v1 whole, which is shorter than its diff:
```python
import jax
import jax.numpy as jnp
from jax import lax
from jax.experimental import pallas as pl
from jax.experimental.pallas import tpu as pltpu
from jax.sharding import PartitionSpec as P

MESH = pl.DeviceIdType.MESH
BLOCK = 256
ZN = 16
CHUNKS = 3
STREAMS = 4
LAST = ((0, 1), (2, 3))


def positions(order):
    places = lax.broadcasted_iota(jnp.int32, order.shape, 1)
    first = jnp.sum(jnp.where(order == 0, places, 0))
    second = jnp.sum(jnp.where(order == 1, places, 0))
    return first, second


def prepare(order_ref, rhs_ref, panel_ref, cand, blocks, factor_v, sem):
    row = lax.axis_index("row")
    nblocks = rhs_ref.shape[0] // BLOCK
    found = positions(order_ref[...])
    copies = []
    for b, place in enumerate(found):
        rows = pl.ds(pl.multiple_of((place % nblocks) * BLOCK, BLOCK), BLOCK)
        copies.append(pltpu.make_async_copy(rhs_ref.at[rows], blocks.at[b], sem.at[b]))
        if b == 1:
            copies.append(pltpu.make_async_copy(panel_ref.at[:, rows], factor_v, sem.at[2]))
    for copy in copies:
        copy.start()
    for copy in copies:
        copy.wait()
    owners = [place // nblocks == row for place in found]
    for b in range(2):
        block = jnp.where(owners[b], blocks[b], jnp.zeros_like(blocks[b]))
        for g in range(2):
            for part in range(2):
                cand[g * 4 + b * 2 + part, 0:128, :] = block[128 * part : 128 * part + 128, 128 * g : 128 * g + 128]
    factor = factor_v[...].astype(jnp.float32)[0:8]
    factor = jnp.where(owners[1], factor, jnp.zeros_like(factor))
    factor = jnp.concatenate([factor[:, 0:128], factor[:, 128:256]], 0).astype(cand.dtype)
    for part in range(8):
        cand[part, 128:144, :] = factor


def exchange(
    cand, piece_ref, g_ref, x_ref, ag_ref,
    rs, ys, yr, total,
    local_sem, rs_send, rs_recv, yx_sem, ag_send, ag_recv, t_sem,
    g_send, g_recv, beta_sem, y_send, y_recv, x_send, x_recv, xy_sem,
):
    row = lax.axis_index("row")
    col = lax.axis_index("col")
    x, yhi, core = row // 4, (row // 2) % 2, row % 2
    ylo, z = col // ZN, col % ZN
    q = x * 2 + core
    width = g_ref.shape[3]
    local = pltpu.make_async_copy

    def at(r, c):
        return {"row": r, "col": c}

    def remote(src, dst, send, recv, device):
        return pltpu.make_async_remote_copy(
            src_ref=src, dst_ref=dst, send_sem=send, recv_sem=recv, device_id=device, device_id_type=MESH
        )

    def peer(offset):
        other = (q + offset) % 8
        return (other // 2) * 4 + yhi * 2 + other % 2

    hi_partner = at(x * 4 + (1 - yhi) * 2 + core, col)
    lo_partner = at(row, (1 - ylo) * ZN + z)
    ring = (at(row, ylo * ZN + (z + 1) % ZN), at(row, ylo * ZN + (z + ZN - 1) % ZN))
    t_row, t_col = col // 2, 2 * row + col % 2
    t_partner = at(t_row, t_col)
    t_self = jnp.logical_and(t_row == row, t_col == col)

    barrier = pltpu.get_barrier_semaphore()

    def greet(device):
        pl.semaphore_signal(barrier, inc=1, device_id=device, device_id_type=MESH)

    for offset in range(1, 8):
        greet(at(peer(offset), col))
    for device in (hi_partner, lo_partner) + ring:
        greet(device)

    @pl.when(jnp.logical_not(t_self))
    def _():
        greet(t_partner)

    pl.semaphore_wait(barrier, 11 + jnp.where(t_self, 0, 1))

    def origin(direction, hops):
        return (z + (ZN - hops if direction == 0 else hops)) % ZN

    def held(stream, place):
        plane = ylo if stream < 3 else 1 - ylo
        return g_ref.at[min(stream, 2), plane * ZN + place]

    def own(chunk):
        return piece_ref.at[:, pl.ds(chunk * width, width)]

    def hop(direction, step, stream):
        place = origin(direction, step - 1)
        dst = held(stream, place)
        src = own(stream) if step == 1 and stream < 3 else dst
        return remote(
            src, dst, g_send.at[direction, step, stream], g_recv.at[direction, step, stream], ring[direction]
        )

    def landed(direction, step, stream):
        dst = held(stream, origin(direction, step))
        remote(
            dst, dst, g_send.at[direction, step, stream], g_recv.at[direction, step, stream], ring[direction]
        ).wait_recv()

    def across(place, chunk):
        dst = g_ref.at[chunk, ylo * ZN + place]
        offset = (place + ZN - z) % ZN
        return remote(dst, dst, y_send.at[offset, chunk], y_recv.at[offset, chunk], lo_partner)

    def across_landed(offset, chunk):
        dst = g_ref.at[chunk, (1 - ylo) * ZN + (z + offset) % ZN]
        remote(dst, dst, y_send.at[offset, chunk], y_recv.at[offset, chunk], lo_partner).wait_recv()

    def streams(direction, step):
        if step < 8:
            return range(STREAMS)
        return LAST[direction] if step == 8 else ()

    beta = remote(own(2), held(2, z), beta_sem.at[0], beta_sem.at[1], lo_partner)
    beta.start()
    for stream in range(3):
        for direction in range(2):
            hop(direction, 1, stream).start()
    for chunk in range(2):
        dst = g_ref.at[chunk, ylo * ZN + z]
        remote(own(chunk), dst, y_send.at[0, chunk], y_recv.at[0, chunk], lo_partner).start()
    keeps = [local(own(chunk), held(chunk, z), local_sem.at[2 + chunk]) for chunk in range(3)]
    for keep in keeps:
        keep.start()

    def scatter(offset):
        other = (q + offset) % 8
        return remote(cand.at[other], rs.at[q], rs_send.at[offset], rs_recv.at[offset], at(peer(offset), col))

    for offset in range(1, 8):
        scatter(offset).start()

    held_beta = held(3, z)
    remote(held_beta, held_beta, beta_sem.at[0], beta_sem.at[1], lo_partner).wait_recv()
    for direction in range(2):
        hop(direction, 1, 3).start()

    def ring_step(step):
        for stream in range(STREAMS):
            for direction in range(2):
                if stream not in streams(direction, step):
                    continue
                landed(direction, step, stream)
                if stream in streams(direction, step + 1):
                    hop(direction, step + 1, stream).start()
                if stream < 2:
                    across(origin(direction, step), stream).start()

    ring_step(1)

    for offset in range(1, 8):
        dst = rs.at[(q + 8 - offset) % 8]
        remote(dst, dst, rs_send.at[offset], rs_recv.at[offset], hi_partner).wait_recv()
    rs[q] = cand[q]
    summed = rs[0].astype(jnp.float32)
    for part in range(1, 8):
        summed = summed + rs[part].astype(jnp.float32)
    ys[...] = summed.astype(ys.dtype)
    swap = remote(ys, yr, yx_sem.at[0], yx_sem.at[1], hi_partner)
    swap.start()

    ring_step(2)

    swap.wait_recv()
    total[...] = (ys[...].astype(jnp.float32) + yr[...].astype(jnp.float32)).astype(total.dtype)

    def gather(offset):
        return remote(
            total.at[pl.ds(0, 128)], ag_ref.at[q], ag_send.at[offset], ag_recv.at[offset], at(peer(offset), col)
        )

    mine = total.at[pl.ds(pl.multiple_of(yhi * 64, 64), 64)]

    def turned(direction_col):
        return x_ref.at[direction_col % ZN, direction_col // ZN, pl.ds(0, 64)]

    turn = remote(mine, turned(t_col), t_sem.at[0], t_sem.at[1], t_partner)
    stay = local(mine, turned(col), t_sem.at[0])

    @pl.when(t_self)
    def _():
        stay.start()

    @pl.when(jnp.logical_not(t_self))
    def _():
        turn.start()

    corner = local(total.at[pl.ds(128, 16)], x_ref.at[z, ylo, pl.ds(64, 16)], local_sem.at[5])
    corner.start()
    for offset in range(1, 8):
        gather(offset).start()
    keep_slice = local(total.at[pl.ds(0, 128)], ag_ref.at[q], local_sem.at[6])
    keep_slice.start()

    ring_step(3)

    @pl.when(t_self)
    def _():
        stay.wait()

    @pl.when(jnp.logical_not(t_self))
    def _():
        dst = turned(col)
        remote(dst, dst, t_sem.at[0], t_sem.at[1], t_partner).wait_recv()
        turn.wait_send()

    corner.wait()
    x_mine, x_other = x_ref.at[z, ylo], x_ref.at[z, 1 - ylo]
    x_swap = remote(x_mine, x_mine, xy_sem.at[0], xy_sem.at[1], lo_partner)
    x_swap.start()

    ring_step(4)

    def x_held(direction, step, place):
        return x_ref.at[place] if step < 8 else x_ref.at[place, direction]

    def x_hop(direction, step):
        ref = x_held(direction, step, origin(direction, step - 1))
        return remote(ref, ref, x_send.at[direction, step], x_recv.at[direction, step], ring[direction])

    def x_step(step):
        for direction in range(2):
            ref = x_held(direction, step, origin(direction, step))
            remote(ref, ref, x_send.at[direction, step], x_recv.at[direction, step], ring[direction]).wait_recv()
            if step < 8:
                x_hop(direction, step + 1).start()

    remote(x_other, x_other, xy_sem.at[0], xy_sem.at[1], lo_partner).wait_recv()
    for direction in range(2):
        x_hop(direction, 1).start()
    ring_step(5)
    x_step(1)
    ring_step(6)
    x_step(2)
    ring_step(7)
    x_step(3)
    ring_step(8)
    for step in range(4, 9):
        x_step(step)

    for offset in range(1, 8):
        dst = ag_ref.at[(q + 8 - offset) % 8]
        remote(dst, dst, ag_send.at[offset], ag_recv.at[offset], hi_partner).wait_recv()
    for offset in range(ZN):
        for chunk in range(2):
            across_landed(offset, chunk)
    for keep in keeps:
        keep.wait()
    keep_slice.wait()
    beta.wait_send()
    swap.wait_send()
    x_swap.wait_send()
    for offset in range(1, 8):
        scatter(offset).wait_send()
        gather(offset).wait_send()
    for offset in range(ZN):
        for chunk in range(2):
            across((z + offset) % ZN, chunk).wait_send()
    for step in range(1, 9):
        for direction in range(2):
            for stream in streams(direction, step):
                hop(direction, step, stream).wait_send()
            x_hop(direction, step).wait_send()


def split3(value):
    parts = []
    for _ in range(3):
        part = value.astype(jnp.bfloat16)
        parts.append(part)
        value = value - part.astype(jnp.float32)
    return parts


def times(matrix, value):
    return sum(jnp.dot(part, value, preferred_element_type=jnp.float32) for part in reversed(split3(matrix)))


def contract_rows(a, b):
    return lax.dot_general(a, b, (((0,), (0,)), ((), ())), preferred_element_type=jnp.float32)


def compute(order_ref, diag_ref, x_ref, ag_ref, g_ref, rhs_ref, work_ref, gram_ref, solved, stacked, spots):
    step = pl.program_id(0)
    tile = rhs_ref.shape[0]
    per_tile = tile // BLOCK
    nblocks = per_tile * pl.num_programs(0)

    @pl.when(step == 0)
    def _():
        first, second = positions(order_ref[...])
        spots[0] = first
        spots[1] = second

        def columns(b):
            sides = [jnp.concatenate([ag_ref[g * 4 + b * 2], ag_ref[g * 4 + b * 2 + 1]], 0) for g in range(2)]
            for parity in range(2):
                for g in range(2):
                    rows = []
                    for core in range(2):
                        for yhi in range(2):
                            c = 2 * ((g * 2 + b) * 4 + yhi * 2 + core) + parity
                            rows.append(x_ref[c % ZN, c // ZN, 0:64])
                    sides.append(jnp.concatenate(rows, 0))
            return jnp.concatenate(sides, 1)

        corner = jnp.concatenate(
            [
                jnp.concatenate(
                    [x_ref[c % ZN, c // ZN, 64:80].astype(jnp.float32)[8 * g : 8 * g + 8] for c in range(2 * ZN)], 0
                )
                for g in range(2)
            ],
            1,
        ).astype(jnp.bfloat16)
        v0 = times(diag_ref[0], columns(0)).astype(jnp.bfloat16)
        left = (columns(1).astype(jnp.float32) - contract_rows(corner, v0)).astype(jnp.bfloat16)
        v1 = times(diag_ref[1], left).astype(jnp.bfloat16)
        solved[0] = v0[:, 0:BLOCK]
        solved[1] = v1[:, 0:BLOCK]
        own0 = v0[:, 0:BLOCK].astype(jnp.float32).reshape(2 * ZN, 8, BLOCK)
        own1 = v1[:, 0:BLOCK].astype(jnp.float32).reshape(2 * ZN, 8, BLOCK)
        stacked[...] = jnp.concatenate([own0, own1], 1).reshape(2 * BLOCK, BLOCK).astype(jnp.bfloat16)
        everything = jnp.concatenate([v0[:, BLOCK:], v1[:, BLOCK:]], 0)
        finished = jnp.concatenate([v0[:, 0:BLOCK], v1[:, 0:BLOCK]], 0)
        gram_ref[...] = contract_rows(everything, finished) / (2 * BLOCK)

    panel = g_ref[0].reshape(2 * BLOCK, tile)
    change = contract_rows(panel, stacked[...])
    base = lax.axis_index("row") * nblocks + step * per_tile
    for part in range(per_tile):
        rows = pl.ds(part * BLOCK, BLOCK)
        fresh = (rhs_ref[rows, :].astype(jnp.float32) - change[part * BLOCK : (part + 1) * BLOCK]).astype(jnp.bfloat16)
        place = base + part
        fresh = jnp.where(place == spots[0], solved[0], fresh)
        work_ref[rows, :] = jnp.where(place == spots[1], solved[1], fresh)


def shards(rhs, panel_columns, diag_inverse, block_order):
    rows, width = rhs.shape
    order = block_order.reshape(1, -1)
    piece = panel_columns.reshape(16, rows)
    bf16 = jnp.bfloat16
    dma = pltpu.SemaphoreType.DMA
    any_space = pl.BlockSpec(memory_space=pl.ANY)
    in_vmem = pl.BlockSpec(memory_space=pltpu.VMEM)
    chunk = rows // CHUNKS
    cand = pl.pallas_call(
        prepare,
        name="prepare",
        out_shape=jax.ShapeDtypeStruct((8, 144, 128), bf16),
        in_specs=[in_vmem, any_space, any_space],
        out_specs=in_vmem,
        scratch_shapes=[pltpu.VMEM((2, BLOCK, width), bf16), pltpu.VMEM((16, BLOCK), bf16), dma((3,))],
        compiler_params=pltpu.CompilerParams(vmem_limit_bytes=60 * 1024 * 1024),
    )(order, rhs, piece)
    g, x, ag = pl.pallas_call(
        exchange,
        name="exchange",
        out_shape=(
            jax.ShapeDtypeStruct((CHUNKS, 2 * ZN, 16, chunk), bf16),
            jax.ShapeDtypeStruct((ZN, 2, 80, 128), bf16),
            jax.ShapeDtypeStruct((8, 128, 128), bf16),
        ),
        in_specs=[in_vmem, any_space],
        out_specs=(any_space, any_space, any_space),
        scratch_shapes=[
            pltpu.VMEM((8, 144, 128), bf16),
            pltpu.VMEM((144, 128), bf16),
            pltpu.VMEM((144, 128), bf16),
            pltpu.VMEM((144, 128), bf16),
            dma((7,)), dma((8,)), dma((8,)), dma((2,)), dma((8,)), dma((8,)), dma((2,)),
            dma((2, 9, STREAMS)), dma((2, 9, STREAMS)), dma((2,)), dma((ZN, 2)), dma((ZN, 2)),
            dma((2, 9)), dma((2, 9)), dma((2,)),
        ],
        compiler_params=pltpu.CompilerParams(
            collective_id=0, has_side_effects=True, vmem_limit_bytes=32 * 1024 * 1024
        ),
    )(cand, piece)
    span = width * 32 // 16
    tile = 512
    fixed = lambda rank: (lambda i: (0,) * rank)
    per_chunk = chunk // tile
    work, gram = pl.pallas_call(
        compute,
        name="compute",
        grid=(rows // tile,),
        out_shape=(
            jax.ShapeDtypeStruct((rows, width), bf16),
            jax.ShapeDtypeStruct((span, width), jnp.float32),
        ),
        in_specs=[
            pl.BlockSpec((1, order.shape[1]), fixed(2)),
            pl.BlockSpec(diag_inverse.shape, fixed(3)),
            pl.BlockSpec(x.shape, fixed(4)),
            pl.BlockSpec(ag.shape, fixed(3)),
            pl.BlockSpec((1, 2 * ZN, 16, tile), lambda i: (i // per_chunk, 0, 0, i % per_chunk)),
            pl.BlockSpec((tile, width), lambda i: (i, 0)),
        ],
        out_specs=(
            pl.BlockSpec((tile, width), lambda i: (i, 0)),
            pl.BlockSpec((span, width), fixed(2)),
        ),
        scratch_shapes=[
            pltpu.VMEM((2, BLOCK, width), bf16),
            pltpu.VMEM((2 * BLOCK, width), bf16),
            pltpu.SMEM((2,), jnp.int32),
        ],
        compiler_params=pltpu.CompilerParams(vmem_limit_bytes=32 * 1024 * 1024),
    )(order, diag_inverse, x, ag, g, rhs)
    return work, gram


def solution(mesh):
    in_specs = (P("row", "col"), P(None, "col", "row"), P(), P())
    out_specs = (P("row", "col"), P("row", "col"))
    return jax.shard_map(shards, mesh=mesh, in_specs=in_specs, out_specs=out_specs, check_vma=False)
```

time: 494 us -> 78.1 us (0.16)
  the two profiles are of different devices: /device:TPU:6 before, /device:TPU:32 now
where the time goes in v1:
time: 78.1 us; the launch traced here: 77.9 us
  Pallas kernels  75.2 us (96%)
  local copies, waits for them, and re-layouts  2.01 us (3%)
    pallas_call x1, Pallas kernels, shards(): pl.pallas_call(exchange, name='exchange', out_shape=(jax.ShapeDtypeStruct...  67.2 us
    pallas_call x1, Pallas kernels, shards(): pl.pallas_call(compute, name='compute', grid=(rows // tile,), out_shape=(...  5.29 us
    pallas_call x1, Pallas kernels, shards(): pl.pallas_call(prepare, name='prepare', out_shape=jax.ShapeDtypeStruct((8...  2.7 us
    unnamed x10, local copies, waits for them, and re-layouts  2.01 us

profile of v1, /device:TPU:32, one launch (start us, length us, event | category | flops | bytes accessed | tf_op | source)
XLA Modules:
  0.0 77.9 jit_solution(10622942076679650784)
XLA Ops:
  0.6 0.0 copy-start
  0.6 0.0 copy-start.4
  0.6 0.0 copy-start.3
  0.7 2.7 %prepare.1.cand = bf16[8,144,128]{2,1,0:T(8,128)(2,1)} custom-call(s32[1,192]{1,0:T(1,128)} %bitcast.4, bf16[3072,256]{1,0:T(8,128)(2,1)} %rhs_ref.3, bf16[16,3072]{1,0:T(8,128)(2,1)} %bitcast.2), custom_call_target="tpu_custom_call" | custom-call | tf_op jit(solution)/shard_map/prepare/pallas_call | solution.py:371
  3.4 0.0 copy-done.3
  3.4 0.0 copy-start.1
  3.4 1.0 %copy-done.1 = bf16[8,144,128]{2,1,0:T(8,128)(2,1)S(1)} copy-done((bf16[8,144,128]{2,1,0:T(8,128)(2,1)S(1)}, bf16[8,144,128]{2,1,0:T(8,128)(2,1)}, u32[]{:S(2)}) %copy-start.1) | copy-done | bytes 294936
  4.3 67.2 %exchange.1 = (bf16[3,32,16,1024]{3,2,1,0:T(8,128)(2,1)S(1)}, bf16[16,2,80,128]{3,2,1,0:T(8,128)(2,1)S(1)}, bf16[8,128,128]{2,1,0:T(8,128)(2,1)S(1)}) custom-call(bf16[8,144,128]{2,1,0:T(8,128)(2,1)S(1)} %copy-done.1, bf16[16,3072]{1,0:T(8,128)(2,1)S(1)} %bitcast.3), custom_call_target="tpu_custom_call" | custom-call | tf_op jit(solution)/shard_map/exchange/pallas_call | solution.py:380
  71.5 0.0 copy-done
  71.6 0.0 copy-done.4
  71.6 0.0 copy-start.2
  71.6 1.0 %copy-done.2 = f32[2,256,256]{2,1,0:T(8,128)S(1)} copy-done((f32[2,256,256]{2,1,0:T(8,128)S(1)}, f32[2,256,256]{2,1,0:T(8,128)}, u32[]{:S(2)}) %copy-start.2) | copy-done | bytes 524312
  72.6 5.3 %compute.1 = (bf16[3072,256]{1,0:T(8,128)(2,1)}, f32[512,256]{1,0:T(8,128)}) custom-call(s32[1,192]{1,0:T(1,128)S(1)} %bitcast.5, f32[2,256,256]{2,1,0:T(8,128)S(1)} %copy-done.2, bf16[16,2,80,128]{3,2,1,0:T(8,128)(2,1)S(1)} %get-tuple-element.5.x_ref, bf16[8,128,128]{2,1,0:T(8,128)(2,1)S(1)} %get-tuple-element.6.ag_ref, ...), custom_call_target="tpu_custom_call" | custom-call | tf_op jit(solution)/shard_map/compute/pallas_call | solution.py:407
Async XLA Ops:
  0.6 70.9 %copy-start = (bf16[3072,256]{1,0:T(8,128)(2,1)S(1)}, bf16[3072,256]{1,0:T(8,128)(2,1)}, u32[]{:S(2)}) copy-start(bf16[3072,256]{1,0:T(8,128)(2,1)} %rhs_ref.3) | copy-start | bytes 4718596
  0.6 70.9 %copy-start.4 = (s32[192]{0:T(256)S(1)}, s32[192]{0:T(256)}, u32[]{:S(2)}) copy-start(s32[192]{0:T(256)} %param.7) | copy-start | bytes 2308
  0.6 2.7 %copy-start.3 = (bf16[2,8,3072]{2,1,0:T(8,128)(2,1)S(1)}, bf16[2,8,3072]{2,1,0:T(8,128)(2,1)}, u32[]{:S(2)}) copy-start(bf16[2,8,3072]{2,1,0:T(8,128)(2,1)} %param.5) | copy-start | bytes 294916
  3.4 1.0 %copy-start.1 = (bf16[8,144,128]{2,1,0:T(8,128)(2,1)S(1)}, bf16[8,144,128]{2,1,0:T(8,128)(2,1)}, u32[]{:S(2)}) copy-start(bf16[8,144,128]{2,1,0:T(8,128)(2,1)} %prepare.1.cand) | copy-start | bytes 884740
  71.6 1.0 %copy-start.2 = (f32[2,256,256]{2,1,0:T(8,128)S(1)}, f32[2,256,256]{2,1,0:T(8,128)}, u32[]{:S(2)}) copy-start(f32[2,256,256]{2,1,0:T(8,128)} %diag_ref.1) | copy-start | bytes 1572868

commit v2 on v0

v2 whole, which is shorter than its diff:
```python
import jax
import jax.numpy as jnp
from jax import lax
from jax.experimental import pallas as pl
from jax.experimental.pallas import tpu as pltpu
from jax.sharding import PartitionSpec as P

MESH = pl.DeviceIdType.MESH
BLOCK = 256
ZN = 16
RN = 16
NEAR, FAR, OTHER, EXTRA = range(4)
STREAMS = (NEAR, FAR, OTHER)
LAST = ((NEAR, EXTRA), (FAR, OTHER))
ADD_AT = 2
EXTRA_AT = 6
EXTRA_EVERY = 2


def exchange(
    order_ref, rhs_ref, piece_ref, g_ref, x_ref, ag_ref,
    rhs_v, panel_v, cand, rs, total,
    local_sem, rs_send, rs_recv, ag_send, ag_recv, t_sem,
    g_send, g_recv, beta_sem, y_send, y_recv,
):
    row = lax.axis_index("row")
    col = lax.axis_index("col")
    ylo, z = col // ZN, col % ZN
    nblocks = rhs_ref.shape[0] // BLOCK
    width = g_ref.shape[3]
    local = pltpu.make_async_copy

    def at(r, c):
        return {"row": r, "col": c}

    def remote(src, dst, send, recv, device):
        return pltpu.make_async_remote_copy(
            src_ref=src, dst_ref=dst, send_sem=send, recv_sem=recv, device_id=device, device_id_type=MESH
        )

    def peer(offset):
        return at((row + offset) % RN, col)

    lo_partner = at(row, (1 - ylo) * ZN + z)
    ring = (at(row, ylo * ZN + (z + 1) % ZN), at(row, ylo * ZN + (z + ZN - 1) % ZN))
    t_row, t_col = col // 2, 2 * row + col % 2
    t_partner = at(t_row, t_col)
    t_self = jnp.logical_and(t_row == row, t_col == col)

    rhs_in = local(rhs_ref, rhs_v, local_sem.at[0])
    panel_in = local(piece_ref, panel_v, local_sem.at[1])
    rhs_in.start()
    panel_in.start()

    barrier = pltpu.get_barrier_semaphore()

    def greet(device):
        pl.semaphore_signal(barrier, inc=1, device_id=device, device_id_type=MESH)

    for offset in range(1, RN):
        greet(peer(offset))
    for device in (lo_partner,) + ring:
        greet(device)

    @pl.when(jnp.logical_not(t_self))
    def _():
        greet(t_partner)

    pl.semaphore_wait(barrier, RN + 2 + jnp.where(t_self, 0, 1))

    def origin(direction, hops):
        return (z + (ZN - hops if direction == 0 else hops)) % ZN

    def held(stream, place):
        plane = 1 - ylo if stream == OTHER else ylo
        if stream == EXTRA:
            return x_ref.at[plane * ZN + place]
        return g_ref.at[0 if stream == NEAR else 1, plane * ZN + place]

    def own(stream):
        return piece_ref.at[:, pl.ds(stream * width, width)]

    def hop(direction, step, stream):
        dst = held(stream, origin(direction, step - 1))
        src = own(stream) if step == 1 and stream in (NEAR, FAR) else dst
        return remote(
            src, dst, g_send.at[direction, step, stream], g_recv.at[direction, step, stream], ring[direction]
        )

    def runs(direction, step, stream):
        return step < 8 or (step == 8 and stream in LAST[direction])

    def across(place, stream):
        dst = held(stream, place)
        src = own(stream) if stream == NEAR and place is z else dst
        offset = (place + ZN - z) % ZN
        return remote(src, dst, y_send.at[offset, stream // EXTRA], y_recv.at[offset, stream // EXTRA], lo_partner)

    def across_landed(offset, stream):
        place = (1 - ylo) * ZN + (z + offset) % ZN
        dst = x_ref.at[place] if stream == EXTRA else g_ref.at[0, place]
        remote(dst, dst, y_send.at[offset, stream // EXTRA], y_recv.at[offset, stream // EXTRA], lo_partner).wait_recv()

    def begin(stream):
        for direction in range(2):
            hop(direction, 1, stream).start()

    def turn_over(step, stream):
        for direction in range(2):
            if not runs(direction, step, stream):
                continue
            place = origin(direction, step)
            dst = held(stream, place)
            remote(
                dst, dst, g_send.at[direction, step, stream], g_recv.at[direction, step, stream], ring[direction]
            ).wait_recv()
            if runs(direction, step + 1, stream):
                hop(direction, step + 1, stream).start()
            if stream in (NEAR, EXTRA):
                across(place, stream).start()

    beta = remote(own(FAR), g_ref.at[1, ylo * ZN + z], beta_sem.at[0], beta_sem.at[1], lo_partner)
    beta.start()
    begin(NEAR)
    across(z, NEAR).start()

    rhs_in.wait()
    masks = [[(order_ref[row * nblocks + p] == b).astype(jnp.float32) for p in range(nblocks)] for b in range(2)]

    def masked(b):
        block = jnp.zeros((BLOCK, rhs_v.shape[1]), jnp.float32)
        for p in range(nblocks):
            block = block + rhs_v[pl.ds(p * BLOCK, BLOCK), :].astype(jnp.float32) * masks[b][p]
        block = block.astype(cand.dtype)
        for g in range(2):
            for part in range(4):
                cand[g * 8 + b * 4 + part, 0:64, :] = block[64 * part : 64 * part + 64, 128 * g : 128 * g + 128]

    masked(0)
    begin(FAR)
    masked(1)
    panel_in.wait()
    factor = jnp.zeros((8, BLOCK), jnp.float32)
    for p in range(nblocks):
        factor = factor + panel_v[:, pl.ds(p * BLOCK, BLOCK)].astype(jnp.float32)[0:8] * masks[1][p]
    factor = jnp.concatenate([factor[:, 0:128], factor[:, 128:256]], 0).astype(cand.dtype)
    for part in range(RN):
        cand[part, 64:80, :] = factor

    def scatter(offset):
        other = (row + offset) % RN
        return remote(cand.at[other], rs.at[row], rs_send.at[offset], rs_recv.at[offset], peer(offset))

    for offset in range(1, RN):
        scatter(offset).start()
    rs[row] = cand[row]
    keeps = [local(own(stream), held(stream, z), local_sem.at[2 + stream]) for stream in (NEAR, FAR)]
    for keep in keeps:
        keep.start()

    theirs = held(OTHER, z)
    remote(theirs, theirs, beta_sem.at[0], beta_sem.at[1], lo_partner).wait_recv()
    begin(OTHER)

    def gather(offset):
        return remote(total.at[pl.ds(0, 64)], ag_ref.at[row], ag_send.at[offset], ag_recv.at[offset], peer(offset))

    def slot(place):
        return x_ref.at[place, pl.ds(0, 64)]

    turn = remote(total.at[pl.ds(0, 64)], slot(t_col), t_sem.at[0], t_sem.at[1], t_partner)
    stay = local(total.at[pl.ds(0, 64)], slot(col), t_sem.at[0])
    corner = local(total.at[pl.ds(64, 16)], x_ref.at[col, pl.ds(64, 16)], local_sem.at[4])
    keep_slice = local(total.at[pl.ds(0, 64)], ag_ref.at[row], local_sem.at[5])

    def add_up():
        for offset in range(1, RN):
            dst = rs.at[(row + RN - offset) % RN]
            remote(dst, dst, rs_send.at[offset], rs_recv.at[offset], lo_partner).wait_recv()
        summed = rs[0].astype(jnp.float32)
        for part in range(1, RN):
            summed = summed + rs[part].astype(jnp.float32)
        total[...] = summed.astype(total.dtype)

        @pl.when(t_self)
        def _():
            stay.start()

        @pl.when(jnp.logical_not(t_self))
        def _():
            turn.start()

        corner.start()
        for offset in range(1, RN):
            gather(offset).start()
        keep_slice.start()

    def begin_extra():
        @pl.when(t_self)
        def _():
            stay.wait()

        @pl.when(jnp.logical_not(t_self))
        def _():
            dst = slot(col)
            remote(dst, dst, t_sem.at[0], t_sem.at[1], t_partner).wait_recv()
            turn.wait_send()

        corner.wait()
        begin(EXTRA)
        across(z, EXTRA).start()

    spot = 0
    extra = 0
    for step in range(1, 9):
        for stream in STREAMS:
            turn_over(step, stream)
            spot += 1
            if spot == ADD_AT:
                add_up()
            if spot == EXTRA_AT:
                begin_extra()
            if spot > EXTRA_AT and (spot - EXTRA_AT) % EXTRA_EVERY == 0 and extra < 8:
                extra += 1
                turn_over(extra, EXTRA)
    while extra < 8:
        extra += 1
        turn_over(extra, EXTRA)

    for offset in range(1, RN):
        dst = ag_ref.at[(row + RN - offset) % RN]
        remote(dst, dst, ag_send.at[offset], ag_recv.at[offset], lo_partner).wait_recv()
    for offset in range(ZN):
        for stream in (NEAR, EXTRA):
            across_landed(offset, stream)
    for keep in keeps:
        keep.wait()
    keep_slice.wait()
    beta.wait_send()
    for offset in range(1, RN):
        scatter(offset).wait_send()
        gather(offset).wait_send()
    for offset in range(ZN):
        for stream in (NEAR, EXTRA):
            across((z + offset) % ZN, stream).wait_send()
    for step in range(1, 9):
        for direction in range(2):
            for stream in STREAMS + (EXTRA,):
                if runs(direction, step, stream):
                    hop(direction, step, stream).wait_send()


def split3(value):
    parts = []
    for _ in range(3):
        part = value.astype(jnp.bfloat16)
        parts.append(part)
        value = value - part.astype(jnp.float32)
    return parts


def times(matrix, value):
    return sum(jnp.dot(part, value, preferred_element_type=jnp.float32) for part in reversed(split3(matrix)))


def contract_rows(a, b):
    return lax.dot_general(a, b, (((0,), (0,)), ((), ())), preferred_element_type=jnp.float32)


def compute(order_ref, diag_ref, x_ref, ag_ref, g_ref, rhs_ref, work_ref, gram_ref, solved, stacked):
    step = pl.program_id(0)
    tile = rhs_ref.shape[0]
    per_tile = tile // BLOCK
    nblocks = per_tile * pl.num_programs(0)

    @pl.when(step == 0)
    def _():

        def columns(b):
            sides = [jnp.concatenate([ag_ref[g * 8 + b * 4 + part] for part in range(4)], 0) for g in range(2)]
            for parity in range(2):
                for g in range(2):
                    sides.append(
                        jnp.concatenate([x_ref[2 * (g * 8 + b * 4 + part) + parity, 0:64] for part in range(4)], 0)
                    )
            return jnp.concatenate(sides, 1)

        corner = jnp.concatenate(
            [
                jnp.concatenate(
                    [x_ref[c, 64:80].astype(jnp.float32)[8 * g : 8 * g + 8] for c in range(2 * ZN)], 0
                )
                for g in range(2)
            ],
            1,
        ).astype(jnp.bfloat16)
        v0 = times(diag_ref[0], columns(0)).astype(jnp.bfloat16)
        left = (columns(1).astype(jnp.float32) - contract_rows(corner, v0)).astype(jnp.bfloat16)
        v1 = times(diag_ref[1], left).astype(jnp.bfloat16)
        solved[0] = v0[:, 0:BLOCK]
        solved[1] = v1[:, 0:BLOCK]
        own0 = v0[:, 0:BLOCK].astype(jnp.float32).reshape(2 * ZN, 8, BLOCK)
        own1 = v1[:, 0:BLOCK].astype(jnp.float32).reshape(2 * ZN, 8, BLOCK)
        stacked[...] = jnp.concatenate([own0, own1], 1).reshape(2 * BLOCK, BLOCK).astype(jnp.bfloat16)
        everything = jnp.concatenate([v0[:, BLOCK:], v1[:, BLOCK:]], 0)
        finished = jnp.concatenate([v0[:, 0:BLOCK], v1[:, 0:BLOCK]], 0)
        gram_ref[...] = contract_rows(everything, finished) / (2 * BLOCK)

    panel = g_ref[0].reshape(2 * BLOCK, tile)
    change = contract_rows(panel, stacked[...])
    base = lax.axis_index("row") * nblocks + step * per_tile
    for part in range(per_tile):
        rows = pl.ds(part * BLOCK, BLOCK)
        fresh = (rhs_ref[rows, :].astype(jnp.float32) - change[part * BLOCK : (part + 1) * BLOCK]).astype(jnp.bfloat16)
        which = order_ref[base + part]
        fresh = jnp.where(which == 0, solved[0], fresh)
        work_ref[rows, :] = jnp.where(which == 1, solved[1], fresh)


def shards(rhs, panel_columns, diag_inverse, block_order):
    rows, width = rhs.shape
    piece = panel_columns.reshape(16, rows)
    bf16 = jnp.bfloat16
    dma = pltpu.SemaphoreType.DMA
    any_space = pl.BlockSpec(memory_space=pl.ANY)
    in_smem = pl.BlockSpec(memory_space=pltpu.SMEM)
    chunk = rows // 2
    g, x, ag = pl.pallas_call(
        exchange,
        name="exchange",
        out_shape=(
            jax.ShapeDtypeStruct((2, 2 * ZN, 16, chunk), bf16),
            jax.ShapeDtypeStruct((2 * ZN, 80, 128), bf16),
            jax.ShapeDtypeStruct((RN, 64, 128), bf16),
        ),
        in_specs=[in_smem, any_space, any_space],
        out_specs=(any_space, any_space, any_space),
        scratch_shapes=[
            pltpu.VMEM((rows, width), bf16),
            pltpu.VMEM((16, rows), bf16),
            pltpu.VMEM((RN, 80, 128), bf16),
            pltpu.VMEM((RN, 80, 128), bf16),
            pltpu.VMEM((80, 128), bf16),
            dma((6,)), dma((RN,)), dma((RN,)), dma((RN,)), dma((RN,)), dma((2,)),
            dma((2, 9, 4)), dma((2, 9, 4)), dma((2,)), dma((ZN, 2)), dma((ZN, 2)),
        ],
        compiler_params=pltpu.CompilerParams(
            collective_id=0, has_side_effects=True, vmem_limit_bytes=32 * 1024 * 1024
        ),
    )(block_order, rhs, piece)
    span = width * 32 // 16
    tile = 512
    fixed = lambda rank: (lambda i: (0,) * rank)
    per_chunk = chunk // tile
    work, gram = pl.pallas_call(
        compute,
        name="compute",
        grid=(rows // tile,),
        out_shape=(
            jax.ShapeDtypeStruct((rows, width), bf16),
            jax.ShapeDtypeStruct((span, width), jnp.float32),
        ),
        in_specs=[
            in_smem,
            pl.BlockSpec(diag_inverse.shape, fixed(3)),
            pl.BlockSpec(x.shape, fixed(3)),
            pl.BlockSpec(ag.shape, fixed(3)),
            pl.BlockSpec((1, 2 * ZN, 16, tile), lambda i: (i // per_chunk, 0, 0, i % per_chunk)),
            pl.BlockSpec((tile, width), lambda i: (i, 0)),
        ],
        out_specs=(
            pl.BlockSpec((tile, width), lambda i: (i, 0)),
            pl.BlockSpec((span, width), fixed(2)),
        ),
        scratch_shapes=[
            pltpu.VMEM((2, BLOCK, width), bf16),
            pltpu.VMEM((2 * BLOCK, width), bf16),
        ],
        compiler_params=pltpu.CompilerParams(vmem_limit_bytes=32 * 1024 * 1024),
    )(block_order, diag_inverse, x, ag, g, rhs)
    return work, gram


def solution(mesh):
    in_specs = (P("row", "col"), P(None, "col", "row"), P(), P())
    out_specs = (P("row", "col"), P("row", "col"))
    return jax.shard_map(shards, mesh=mesh, in_specs=in_specs, out_specs=out_specs, check_vma=False)
```

time: 494 us -> 70.3 us (0.14)
  waiting for transfers between devices: 443 us -> 0 us
  Pallas kernels: 0 us -> 65.3 us
  between operations: 19.6 us -> 0.66 us
  matrix products: 12.5 us -> 0 us
  local copies, waits for them, and re-layouts: 13.8 us -> 2.98 us
    psum x2 -> x0, waiting for transfers between devices: 297 us -> none  [broadcast(): return lax.psum(kept, axis)]
    all_gather x3 -> x0, waiting for transfers between devices: 146 us -> none  [the longest x1 146 us: shards(): everything = lax.all_gather(finished, 'col', axis=1, tiled=True)]
    pallas_call x0 -> x2, Pallas kernels: none -> 65.3 us  [the longest x1 59.4 us: shards(): pl.pallas_call(exchange, name='exchange', out_shape=(jax.ShapeDtypeStruct...]
    dot_general x5 -> x0, matrix products: 12.5 us -> none  [the longest x2 7.29 us: contract_rows(): lax.dot_general(factor, solved, (((0,), (0,)), ((), ())), preferred_eleme...]
  transfers between devices with their start and end apart: 5 -> 0, of which waited for: 3 -> 0; matrix products, arithmetic and copies ran while one was open for 4% -> 0% of each run, Pallas kernels for 0% -> 0%
where the time goes in v2:
time: 70.3 us; the launch traced here: 68.9 us
  Pallas kernels  65.3 us (93%)
  local copies, waits for them, and re-layouts  2.98 us (4%)
    pallas_call x1, Pallas kernels, shards(): pl.pallas_call(exchange, name='exchange', out_shape=(jax.ShapeDtypeStruct...  59.4 us
    pallas_call x1, Pallas kernels, shards(): pl.pallas_call(compute, name='compute', grid=(rows // tile,), out_shape=(...  5.86 us
    unnamed x8, local copies, waits for them, and re-layouts  2.98 us

profile of v2, /device:TPU:6, one launch (start us, length us, event | category | flops | bytes accessed | tf_op | source)
XLA Modules:
  0.0 68.9 jit_solution(2535744808395206423)
XLA Ops:
  0.6 0.0 copy-start
  0.6 1.4 %copy-done = bf16[3072,256]{1,0:T(8,128)(2,1)S(1)} copy-done((bf16[3072,256]{1,0:T(8,128)(2,1)S(1)}, bf16[3072,256]{1,0:T(8,128)(2,1)}, u32[]{:S(2)}) %copy-start) | copy-done | bytes 1572888
  2.0 0.0 copy-start.2
  2.0 0.9 %copy-done.2 = bf16[2,8,3072]{2,1,0:T(8,128)(2,1)S(1)} copy-done((bf16[2,8,3072]{2,1,0:T(8,128)(2,1)S(1)}, bf16[2,8,3072]{2,1,0:T(8,128)(2,1)}, u32[]{:S(2)}) %copy-start.2) | copy-done | bytes 98328
  2.9 0.0 copy-start.3
  2.9 0.7 copy-done.3
  3.6 0.0 copy-start.1
  3.6 59.4 %exchange.1 = (bf16[2,32,16,1536]{3,2,1,0:T(8,128)(2,1)S(1)}, bf16[32,80,128]{2,1,0:T(8,128)(2,1)S(1)}, bf16[16,64,128]{2,1,0:T(8,128)(2,1)S(1)}) custom-call(s32[192]{0:T(256)S(1)} %copy-done.3, bf16[3072,256]{1,0:T(8,128)(2,1)S(1)} %copy-done, bf16[16,3072]{1,0:T(8,128)(2,1)S(1)} %bitcast.1), custom_call_target="tpu_custom_call" | custom-call | tf_op jit(solution)/shard_map/exchange/pallas_call | solution.py:328
  63.0 0.0 copy-done.1
  63.1 5.9 %compute.1 = (bf16[3072,256]{1,0:T(8,128)(2,1)}, f32[512,256]{1,0:T(8,128)}) custom-call(s32[192]{0:T(256)S(1)} %copy-done.3, f32[2,256,256]{2,1,0:T(8,128)S(1)} %copy-done.1, bf16[32,80,128]{2,1,0:T(8,128)(2,1)S(1)} %get-tuple-element.5.x_ref, bf16[16,64,128]{2,1,0:T(8,128)(2,1)S(1)} %get-tuple-element.6.ag_ref, ...), custom_call_target="tpu_custom_call" | custom-call | tf_op jit(solution)/shard_map/compute/pallas_call | solution.py:355
Async XLA Ops:
  0.6 1.4 %copy-start = (bf16[3072,256]{1,0:T(8,128)(2,1)S(1)}, bf16[3072,256]{1,0:T(8,128)(2,1)}, u32[]{:S(2)}) copy-start(bf16[3072,256]{1,0:T(8,128)(2,1)} %rhs_ref.3) | copy-start | bytes 4718596
  2.0 0.9 %copy-start.2 = (bf16[2,8,3072]{2,1,0:T(8,128)(2,1)S(1)}, bf16[2,8,3072]{2,1,0:T(8,128)(2,1)}, u32[]{:S(2)}) copy-start(bf16[2,8,3072]{2,1,0:T(8,128)(2,1)} %param.5) | copy-start | bytes 294916
  2.9 0.7 copy-start.3
  3.6 59.4 %copy-start.1 = (f32[2,256,256]{2,1,0:T(8,128)S(1)}, f32[2,256,256]{2,1,0:T(8,128)}, u32[]{:S(2)}) copy-start(f32[2,256,256]{2,1,0:T(8,128)} %diag_ref.1) | copy-start | bytes 1572868

commit v3 on v2

v3 whole, which is shorter than its diff:
```python
import functools

import jax
import jax.numpy as jnp
from jax import lax
from jax.experimental import pallas as pl
from jax.experimental.pallas import tpu as pltpu
from jax.sharding import PartitionSpec as P

MESH = pl.DeviceIdType.MESH
BLOCK = 256
ZN = 16
RN = 16
NEAR, FAR, OTHER = STREAMS = range(3)
LAST = ((NEAR,), (FAR, OTHER))
STEP = 4.1
FIRST = {NEAR: 3.5, FAR: 4.5, OTHER: 6.0}
ADD_AT = 9.5
EXTRA_AT = 17.0
EXTRA_STEP = 5.0
SOLVE_AT = 33.0
REACH = 4
TILE = 512


def split3(value):
    parts = []
    for _ in range(3):
        part = value.astype(jnp.bfloat16)
        parts.append(part)
        value = value - part.astype(jnp.float32)
    return parts


def times(matrix, value):
    return sum(jnp.dot(part, value, preferred_element_type=jnp.float32) for part in reversed(split3(matrix)))


def contract_rows(a, b):
    return lax.dot_general(a, b, (((0,), (0,)), ((), ())), preferred_element_type=jnp.float32)


def whole(
    order_ref, diag_ref, rhs_ref, piece_ref, work_ref, gram_ref,
    rhs_v, panel_v, diag_v, g_ref, x_ref, ag_ref, cand, rs, total, solved, stacked, work_v, gram_v,
    local_sem, rs_send, rs_recv, ag_send, ag_recv, t_sem,
    g_send, g_recv, beta_sem, y_send, y_recv, x_send, x_recv, out_sem,
):
    row = lax.axis_index("row")
    col = lax.axis_index("col")
    ylo, z = col // ZN, col % ZN
    nblocks = rhs_ref.shape[0] // BLOCK
    width = g_ref.shape[3]
    local = pltpu.make_async_copy

    def at(r, c):
        return {"row": r, "col": c}

    def remote(src, dst, send, recv, device):
        return pltpu.make_async_remote_copy(
            src_ref=src, dst_ref=dst, send_sem=send, recv_sem=recv, device_id=device, device_id_type=MESH
        )

    def peer(offset):
        return at((row + offset) % RN, col)

    lo_partner = at(row, (1 - ylo) * ZN + z)
    ring = (at(row, ylo * ZN + (z + 1) % ZN), at(row, ylo * ZN + (z + ZN - 1) % ZN))
    reaches = [
        (at(row, ylo * ZN + (z + far) % ZN), at(row, ylo * ZN + (z + ZN - far) % ZN)) for far in range(1, REACH + 1)
    ]
    t_row, t_col = col // 2, 2 * row + col % 2
    t_partner = at(t_row, t_col)
    t_self = jnp.logical_and(t_row == row, t_col == col)

    rhs_in = local(rhs_ref, rhs_v, local_sem.at[0])
    panel_in = local(piece_ref, panel_v, local_sem.at[1])
    rhs_in.start()
    panel_in.start()
    diag_in = local(diag_ref, diag_v, local_sem.at[6])
    diag_in.start()

    barrier = pltpu.get_barrier_semaphore()

    def greet(device):
        pl.semaphore_signal(barrier, inc=1, device_id=device, device_id_type=MESH)

    for offset in range(1, RN):
        greet(peer(offset))
    greet(lo_partner)
    for pair in reaches:
        for device in pair:
            greet(device)

    @pl.when(jnp.logical_not(t_self))
    def _():
        greet(t_partner)

    pl.semaphore_wait(barrier, RN + 2 * REACH + jnp.where(t_self, 0, 1))

    def origin(direction, hops):
        return (z + (ZN - hops if direction == 0 else hops)) % ZN

    def held(stream, place):
        plane = 1 - ylo if stream == OTHER else ylo
        return g_ref.at[0 if stream == NEAR else 1, plane * ZN + place]

    def own(stream):
        return piece_ref.at[:, pl.ds(stream * width, width)]

    def hop(direction, step, stream):
        dst = held(stream, origin(direction, step - 1))
        src = own(stream) if step == 1 and stream in (NEAR, FAR) else dst
        return remote(
            src, dst, g_send.at[direction, step, stream], g_recv.at[direction, step, stream], ring[direction]
        )

    def runs(direction, step, stream):
        return step < 8 or (step == 8 and stream in LAST[direction])

    def across(place, extra):
        place_in_col = ylo * ZN + place
        dst = x_ref.at[place_in_col] if extra else g_ref.at[0, place_in_col]
        offset = (place + ZN - z) % ZN
        return remote(dst, dst, y_send.at[offset, extra], y_recv.at[offset, extra], lo_partner)

    def across_landed(offset, extra):
        place_in_col = (1 - ylo) * ZN + (z + offset) % ZN
        dst = x_ref.at[place_in_col] if extra else g_ref.at[0, place_in_col]
        remote(dst, dst, y_send.at[offset, extra], y_recv.at[offset, extra], lo_partner).wait_recv()

    def begin(stream):
        for direction in range(2):
            hop(direction, 1, stream).start()

    def turn_over(step, stream):
        for direction in range(2):
            if not runs(direction, step, stream):
                continue
            place = origin(direction, step)
            dst = held(stream, place)
            remote(
                dst, dst, g_send.at[direction, step, stream], g_recv.at[direction, step, stream], ring[direction]
            ).wait_recv()
            if runs(direction, step + 1, stream):
                hop(direction, step + 1, stream).start()
            if stream == NEAR:
                across(place, 0).start()

    def x_far(direction, hops):
        return range(hops + 1, min(hops + REACH, 7 + (direction == 0)) + 1)

    def x_hop(direction, hops, reach):
        dst = x_ref.at[ylo * ZN + origin(direction, hops)]
        to = reaches[reach - hops - 1][direction]
        return remote(dst, dst, x_send.at[direction, reach], x_recv.at[direction, reach], to)

    def x_begin(hops):
        for reach in range(hops + REACH, hops, -1):
            for direction in range(2):
                if reach in x_far(direction, hops):
                    x_hop(direction, hops, reach).start()

    def x_landed(hops):
        for direction in range(2):
            if hops <= 7 + (direction == 0):
                dst = x_ref.at[ylo * ZN + origin(direction, hops)]
                remote(
                    dst, dst, x_send.at[direction, hops], x_recv.at[direction, hops], ring[direction]
                ).wait_recv()
                if hops == REACH:
                    for reach in reversed(x_far(direction, hops)):
                        x_hop(direction, hops, reach).start()
                across(origin(direction, hops), 1).start()

    beta = remote(own(FAR), g_ref.at[1, ylo * ZN + z], beta_sem.at[0], beta_sem.at[1], lo_partner)
    beta.start()
    begin(NEAR)
    begin(FAR)
    remote(own(NEAR), held(NEAR, z), y_send.at[0, 0], y_recv.at[0, 0], lo_partner).start()

    rhs_in.wait()
    masks = [[(order_ref[row * nblocks + p] == b).astype(jnp.float32) for p in range(nblocks)] for b in range(2)]

    def masked(part, carry):
        for g in range(2):
            lanes = pl.ds(128 * g, 128)
            sums = [jnp.zeros((64, 128), jnp.float32)] * 2
            for p in range(nblocks):
                rows = pl.ds(pl.multiple_of(p * BLOCK + part * 64, 64), 64)
                value = rhs_v[rows, lanes].astype(jnp.float32)
                sums = [total_ + value * masks[b][p] for b, total_ in enumerate(sums)]
            for b in range(2):
                cand[g * 8 + b * 4 + part, 0:64, :] = sums[b].astype(cand.dtype)
        return carry

    lax.fori_loop(0, 4, masked, 0)
    panel_in.wait()
    factor = jnp.zeros((8, BLOCK), jnp.float32)
    for p in range(nblocks):
        factor = factor + panel_v[:, pl.ds(p * BLOCK, BLOCK)].astype(jnp.float32)[0:8] * masks[1][p]
    factor = jnp.concatenate([factor[:, 0:128], factor[:, 128:256]], 0).astype(cand.dtype)
    for part in range(RN):
        cand[part, 64:80, :] = factor

    def scatter(offset):
        other = (row + offset) % RN
        return remote(cand.at[other], rs.at[row], rs_send.at[offset], rs_recv.at[offset], peer(offset))

    for offset in range(1, RN):
        scatter(offset).start()
    rs[row] = cand[row]
    keeps = [local(own(stream), held(stream, z), local_sem.at[2 + stream]) for stream in (NEAR, FAR)]
    for keep in keeps:
        keep.start()

    theirs = held(OTHER, z)
    remote(theirs, theirs, beta_sem.at[0], beta_sem.at[1], lo_partner).wait_recv()
    begin(OTHER)

    def gather(offset):
        return remote(total.at[pl.ds(0, 64)], ag_ref.at[row], ag_send.at[offset], ag_recv.at[offset], peer(offset))

    def slot(place):
        return x_ref.at[place, pl.ds(0, 64)]

    turn = remote(total.at[pl.ds(0, 64)], slot(t_col), t_sem.at[0], t_sem.at[1], t_partner)
    stay = local(total.at[pl.ds(0, 64)], slot(col), t_sem.at[0])
    corner = local(total.at[pl.ds(64, 16)], x_ref.at[col, pl.ds(64, 16)], local_sem.at[4])
    keep_slice = local(total.at[pl.ds(0, 64)], ag_ref.at[row], local_sem.at[5])

    def add_up():
        for offset in range(1, RN):
            dst = rs.at[(row + RN - offset) % RN]
            remote(dst, dst, rs_send.at[offset], rs_recv.at[offset], lo_partner).wait_recv()
        summed = rs[0].astype(jnp.float32)
        for part in range(1, RN):
            summed = summed + rs[part].astype(jnp.float32)
        total[...] = summed.astype(total.dtype)

        @pl.when(t_self)
        def _():
            stay.start()

        @pl.when(jnp.logical_not(t_self))
        def _():
            turn.start()

        corner.start()
        for offset in range(1, RN):
            gather(offset).start()
        keep_slice.start()

    def begin_extra():
        @pl.when(t_self)
        def _():
            stay.wait()

        @pl.when(jnp.logical_not(t_self))
        def _():
            dst = slot(col)
            remote(dst, dst, t_sem.at[0], t_sem.at[1], t_partner).wait_recv()
            turn.wait_send()

        corner.wait()
        x_begin(0)
        across(z, 1).start()

    def solve():
        for offset in range(1, RN):
            dst = ag_ref.at[(row + RN - offset) % RN]
            remote(dst, dst, ag_send.at[offset], ag_recv.at[offset], lo_partner).wait_recv()
        keep_slice.wait()
        diag_in.wait()
        for offset in range(ZN):
            across_landed(offset, 1)

        def columns(b):
            sides = [jnp.concatenate([ag_ref[g * 8 + b * 4 + part] for part in range(4)], 0) for g in range(2)]
            for parity in range(2):
                for g in range(2):
                    sides.append(
                        jnp.concatenate([x_ref[2 * (g * 8 + b * 4 + part) + parity, 0:64] for part in range(4)], 0)
                    )
            return jnp.concatenate(sides, 1)

        corner_rows = jnp.concatenate(
            [
                jnp.concatenate([x_ref[c, 64:80].astype(jnp.float32)[8 * g : 8 * g + 8] for c in range(2 * ZN)], 0)
                for g in range(2)
            ],
            1,
        ).astype(jnp.bfloat16)
        v0 = times(diag_v[0], columns(0)).astype(jnp.bfloat16)
        left = (columns(1).astype(jnp.float32) - contract_rows(corner_rows, v0)).astype(jnp.bfloat16)
        v1 = times(diag_v[1], left).astype(jnp.bfloat16)
        solved[0] = v0[:, 0:BLOCK]
        solved[1] = v1[:, 0:BLOCK]
        own0 = v0[:, 0:BLOCK].astype(jnp.float32).reshape(2 * ZN, 8, BLOCK)
        own1 = v1[:, 0:BLOCK].astype(jnp.float32).reshape(2 * ZN, 8, BLOCK)
        stacked[...] = jnp.concatenate([own0, own1], 1).reshape(2 * BLOCK, BLOCK).astype(jnp.bfloat16)
        everything = jnp.concatenate([v0[:, BLOCK:], v1[:, BLOCK:]], 0)
        finished = jnp.concatenate([v0[:, 0:BLOCK], v1[:, 0:BLOCK]], 0)
        gram_v[...] = contract_rows(everything, finished) / (2 * BLOCK)

    def update(half):
        outs = []
        for tile in range(width // TILE):
            panel = g_ref[half, :, :, pl.ds(tile * TILE, TILE)].reshape(2 * BLOCK, TILE)
            change = contract_rows(panel, stacked[...])
            for part in range(TILE // BLOCK):
                p = half * (width // BLOCK) + tile * (TILE // BLOCK) + part
                rows = pl.ds(p * BLOCK, BLOCK)
                fresh = rhs_v[rows, :].astype(jnp.float32) - change[part * BLOCK : (part + 1) * BLOCK]
                fresh = fresh.astype(jnp.bfloat16)
                which = order_ref[row * nblocks + p]
                fresh = jnp.where(which == 0, solved[0], fresh)
                work_v[rows, :] = jnp.where(which == 1, solved[1], fresh)
            rows = pl.ds(half * width + tile * TILE, TILE)
            out = local(work_v.at[rows], work_ref.at[rows], out_sem.at[half * (width // TILE) + tile])
            out.start()
            outs.append(out)
        return outs

    outs = []

    def solve_and_write():
        solve()
        out = local(gram_v, gram_ref, out_sem.at[2 * (width // TILE)])
        out.start()
        outs.append(out)

    plan = [
        (FIRST[stream] + STEP * (step - 1), functools.partial(turn_over, step, stream))
        for step in range(1, 9)
        for stream in STREAMS
    ]
    plan += [(ADD_AT, add_up), (EXTRA_AT, begin_extra), (SOLVE_AT, solve_and_write)]
    plan += [
        (EXTRA_AT + EXTRA_STEP * (1 + (hops - 1) // REACH), functools.partial(x_landed, hops))
        for hops in (4, 1, 2, 3, 8, 5, 6, 7)
    ]
    for _, act in sorted(plan, key=lambda item: item[0]):
        act()
    for keep in keeps:
        keep.wait()
    outs += update(1)
    for offset in range(ZN):
        across_landed(offset, 0)
    outs += update(0)

    for out in outs:
        out.wait()
    beta.wait_send()
    for offset in range(1, RN):
        scatter(offset).wait_send()
        gather(offset).wait_send()
    for offset in range(ZN):
        for extra in range(2):
            across((z + offset) % ZN, extra).wait_send()
    for step in range(1, 9):
        for direction in range(2):
            for stream in STREAMS:
                if runs(direction, step, stream):
                    hop(direction, step, stream).wait_send()
    for hops in (0, REACH):
        for direction in range(2):
            for reach in x_far(direction, hops):
                x_hop(direction, hops, reach).wait_send()


def shards(rhs, panel_columns, diag_inverse, block_order):
    rows, width = rhs.shape
    piece = panel_columns.reshape(16, rows)
    bf16 = jnp.bfloat16
    dma = pltpu.SemaphoreType.DMA
    any_space = pl.BlockSpec(memory_space=pl.ANY)
    in_smem = pl.BlockSpec(memory_space=pltpu.SMEM)
    half = rows // 2
    span = width * 32 // RN
    return pl.pallas_call(
        whole,
        name="whole",
        out_shape=(
            jax.ShapeDtypeStruct((rows, width), bf16),
            jax.ShapeDtypeStruct((span, width), jnp.float32),
        ),
        in_specs=[in_smem, any_space, any_space, any_space],
        out_specs=(any_space, any_space),
        scratch_shapes=[
            pltpu.VMEM((rows, width), bf16),
            pltpu.VMEM((16, rows), bf16),
            pltpu.VMEM(diag_inverse.shape, jnp.float32),
            pltpu.VMEM((2, 2 * ZN, 16, half), bf16),
            pltpu.VMEM((2 * ZN, 80, 128), bf16),
            pltpu.VMEM((RN, 64, 128), bf16),
            pltpu.VMEM((RN, 80, 128), bf16),
            pltpu.VMEM((RN, 80, 128), bf16),
            pltpu.VMEM((80, 128), bf16),
            pltpu.VMEM((2, BLOCK, width), bf16),
            pltpu.VMEM((2 * BLOCK, width), bf16),
            pltpu.VMEM((rows, width), bf16),
            pltpu.VMEM((span, width), jnp.float32),
            dma((7,)), dma((RN,)), dma((RN,)), dma((RN,)), dma((RN,)), dma((2,)),
            dma((2, 9, 3)), dma((2, 9, 3)), dma((2,)), dma((ZN, 2)), dma((ZN, 2)),
            dma((2, 9)), dma((2, 9)), dma((2 * (half // TILE) + 1,)),
        ],
        compiler_params=pltpu.CompilerParams(
            collective_id=0, has_side_effects=True, vmem_limit_bytes=56 * 1024 * 1024
        ),
    )(block_order, diag_inverse, rhs, piece)


def solution(mesh):
    in_specs = (P("row", "col"), P(None, "col", "row"), P(), P())
    out_specs = (P("row", "col"), P("row", "col"))
    return jax.shard_map(shards, mesh=mesh, in_specs=in_specs, out_specs=out_specs, check_vma=False)
```

time: 70.3 us -> 66.3 us (0.943); the launches traced: 68.9 us -> 66.1 us
  Pallas kernels: 65.3 us -> 62 us
    pallas_call x2 -> x1, Pallas kernels: 65.3 us -> 62 us  [shards(): pl.pallas_call(whole, name='whole', out_shape=(jax.ShapeDtypeStruct((rows...]
    unnamed x8 -> x4, local copies, waits for them, and re-layouts: 2.98 us -> 3.51 us
where the time goes in v3:
time: 66.3 us; the launch traced here: 66.1 us
  Pallas kernels  62 us (94%)
  local copies, waits for them, and re-layouts  3.51 us (5%)
    pallas_call x1, Pallas kernels, shards(): pl.pallas_call(whole, name='whole', out_shape=(jax.ShapeDtypeStruct((rows...  62 us
    unnamed x4, local copies, waits for them, and re-layouts  3.51 us

profile of v3, /device:TPU:6, one launch (start us, length us, event | category | flops | bytes accessed | tf_op | source)
XLA Modules:
  0.0 66.1 jit_solution(3325895218761301040)
XLA Ops:
  0.6 62.0 %whole.1 = (bf16[3072,256]{1,0:T(8,128)(2,1)}, f32[512,256]{1,0:T(8,128)}) custom-call(s32[192]{0:T(256)} %order_ref.1, f32[2,256,256]{2,1,0:T(8,128)} %diag_ref.1, bf16[3072,256]{1,0:T(8,128)(2,1)} %rhs_ref.1, bf16[16,3072]{1,0:T(8,128)(2,1)} %bitcast.1), custom_call_target="tpu_custom_call" | custom-call | tf_op jit(solution)/shard_map/whole/pallas_call | solution.py:381
  62.6 0.0 copy-start
  62.6 2.7 %copy.8 = bf16[3072,256]{1,0:T(8,128)(2,1)} copy(bf16[3072,256]{1,0:T(8,128)(2,1)} %get-tuple-element.4) | data formatting | bytes 3145728
  65.3 0.0 copy-done
  65.3 0.8 %copy.9 = f32[512,256]{1,0:T(8,128)} copy(f32[512,256]{1,0:T(8,128)S(1)} %copy-done) | data formatting | bytes 1048576
Async XLA Ops:
  62.6 2.7 %copy-start = (f32[512,256]{1,0:T(8,128)S(1)}, f32[512,256]{1,0:T(8,128)}, u32[]{:S(2)}) copy-start(f32[512,256]{1,0:T(8,128)} %get-tuple-element.5) | copy-start | bytes 1572868

commit v4 on v3

--- a/solution.py
+++ b/solution.py
@@ -17,9 +17,10 @@
 FIRST = {NEAR: 3.5, FAR: 4.5, OTHER: 6.0}
 ADD_AT = 9.5
 EXTRA_AT = 17.0
-EXTRA_STEP = 5.0
+EXTRA_STEP = 4.5
+SHARE_AT = 18.0
 SOLVE_AT = 33.0
-REACH = 4
+REACH = 3
 TILE = 512
 
 
@@ -42,8 +43,8 @@
 
 def whole(
     order_ref, diag_ref, rhs_ref, piece_ref, work_ref, gram_ref,
-    rhs_v, panel_v, diag_v, g_ref, x_ref, ag_ref, cand, rs, total, solved, stacked, work_v, gram_v,
-    local_sem, rs_send, rs_recv, ag_send, ag_recv, t_sem,
+    rhs_v, panel_v, diag_v, g_ref, x_ref, ag_ref, cand, pair, rs, total, solved, stacked, work_v, gram_v,
+    local_sem, pair_sem, rs_send, rs_recv, ag_send, ag_recv, t_sem,
     g_send, g_recv, beta_sem, y_send, y_recv, x_send, x_recv, out_sem,
 ):
     row = lax.axis_index("row")
@@ -61,8 +62,12 @@
             src_ref=src, dst_ref=dst, send_sem=send, recv_sem=recv, device_id=device, device_id_type=MESH
         )
 
+    core, chip = row % 2, row // 2
+
     def peer(offset):
-        return at((row + offset) % RN, col)
+        return at((chip + offset) % 8 * 2 + core, col)
+
+    sibling = at(chip * 2 + 1 - core, col)
 
     lo_partner = at(row, (1 - ylo) * ZN + z)
     ring = (at(row, ylo * ZN + (z + 1) % ZN), at(row, ylo * ZN + (z + ZN - 1) % ZN))
@@ -85,18 +90,19 @@
     def greet(device):
         pl.semaphore_signal(barrier, inc=1, device_id=device, device_id_type=MESH)
 
-    for offset in range(1, RN):
+    for offset in range(1, 8):
         greet(peer(offset))
+    greet(sibling)
     greet(lo_partner)
-    for pair in reaches:
-        for device in pair:
+    for both_ways in reaches:
+        for device in both_ways:
             greet(device)
 
     @pl.when(jnp.logical_not(t_self))
     def _():
         greet(t_partner)
 
-    pl.semaphore_wait(barrier, RN + 2 * REACH + jnp.where(t_self, 0, 1))
+    pl.semaphore_wait(barrier, 9 + 2 * REACH + jnp.where(t_self, 0, 1))
 
     def origin(direction, hops):
         return (z + (ZN - hops if direction == 0 else hops)) % ZN
@@ -168,7 +174,7 @@
                 remote(
                     dst, dst, x_send.at[direction, hops], x_recv.at[direction, hops], ring[direction]
                 ).wait_recv()
-                if hops == REACH:
+                if hops in (REACH, 2 * REACH):
                     for reach in reversed(x_far(direction, hops)):
                         x_hop(direction, hops, reach).start()
                 across(origin(direction, hops), 1).start()
@@ -191,7 +197,7 @@
                 value = rhs_v[rows, lanes].astype(jnp.float32)
                 sums = [total_ + value * masks[b][p] for b, total_ in enumerate(sums)]
             for b in range(2):
-                cand[g * 8 + b * 4 + part, 0:64, :] = sums[b].astype(cand.dtype)
+                cand[part % 2 * 8 + g * 4 + b * 2 + part // 2, 0:64, :] = sums[b].astype(cand.dtype)
         return carry
 
     lax.fori_loop(0, 4, masked, 0)
@@ -203,13 +209,11 @@
     for part in range(RN):
         cand[part, 64:80, :] = factor
 
-    def scatter(offset):
-        other = (row + offset) % RN
-        return remote(cand.at[other], rs.at[row], rs_send.at[offset], rs_recv.at[offset], peer(offset))
-
-    for offset in range(1, RN):
-        scatter(offset).start()
-    rs[row] = cand[row]
+    def side(ref, which):
+        return ref.at[pl.ds(pl.multiple_of(which * 8, 8), 8)]
+
+    halves = remote(side(cand, 1 - core), pair, pair_sem.at[0], pair_sem.at[1], sibling)
+    halves.start()
     keeps = [local(own(stream), held(stream, z), local_sem.at[2 + stream]) for stream in (NEAR, FAR)]
     for keep in keeps:
         keep.start()
@@ -218,8 +222,23 @@
     remote(theirs, theirs, beta_sem.at[0], beta_sem.at[1], lo_partner).wait_recv()
     begin(OTHER)
 
+    def scatter(offset):
+        return remote(
+            pair.at[(chip + offset) % 8], rs.at[chip], rs_send.at[offset], rs_recv.at[offset], peer(offset)
+        )
+
+    halves.wait()
+    for part in range(8):
+        both = pair[part].astype(jnp.float32) + cand[core * 8 + part].astype(jnp.float32)
+        pair[part] = both.astype(pair.dtype)
+    for offset in range(1, 8):
+        scatter(offset).start()
+    rs[chip] = pair[chip]
+
     def gather(offset):
-        return remote(total.at[pl.ds(0, 64)], ag_ref.at[row], ag_send.at[offset], ag_recv.at[offset], peer(offset))
+        return remote(
+            total.at[pl.ds(0, 64)], ag_ref.at[core * 8 + chip], ag_send.at[offset], ag_recv.at[offset], peer(offset)
+        )
 
     def slot(place):
         return x_ref.at[place, pl.ds(0, 64)]
@@ -227,14 +246,14 @@
     turn = remote(total.at[pl.ds(0, 64)], slot(t_col), t_sem.at[0], t_sem.at[1], t_partner)
     stay = local(total.at[pl.ds(0, 64)], slot(col), t_sem.at[0])
     corner = local(total.at[pl.ds(64, 16)], x_ref.at[col, pl.ds(64, 16)], local_sem.at[4])
-    keep_slice = local(total.at[pl.ds(0, 64)], ag_ref.at[row], local_sem.at[5])
+    keep_slice = local(total.at[pl.ds(0, 64)], ag_ref.at[core * 8 + chip], local_sem.at[5])
 
     def add_up():
-        for offset in range(1, RN):
-            dst = rs.at[(row + RN - offset) % RN]
+        for offset in range(1, 8):
+            dst = rs.at[(chip + 8 - offset) % 8]
             remote(dst, dst, rs_send.at[offset], rs_recv.at[offset], lo_partner).wait_recv()
         summed = rs[0].astype(jnp.float32)
-        for part in range(1, RN):
+        for part in range(1, 8):
             summed = summed + rs[part].astype(jnp.float32)
         total[...] = summed.astype(total.dtype)
 
@@ -247,9 +266,18 @@
             turn.start()
 
         corner.start()
-        for offset in range(1, RN):
+        for offset in range(1, 8):
             gather(offset).start()
         keep_slice.start()
+
+    share = remote(side(ag_ref, core), side(ag_ref, core), pair_sem.at[2], pair_sem.at[3], sibling)
+
+    def share_blocks():
+        for offset in range(1, 8):
+            dst = ag_ref.at[core * 8 + (chip + 8 - offset) % 8]
+            remote(dst, dst, ag_send.at[offset], ag_recv.at[offset], lo_partner).wait_recv()
+        keep_slice.wait()
+        share.start()
 
     def begin_extra():
         @pl.when(t_self)
@@ -267,16 +295,14 @@
         across(z, 1).start()
 
     def solve():
-        for offset in range(1, RN):
-            dst = ag_ref.at[(row + RN - offset) % RN]
-            remote(dst, dst, ag_send.at[offset], ag_recv.at[offset], lo_partner).wait_recv()
-        keep_slice.wait()
+        dst = side(ag_ref, 1 - core)
+        remote(dst, dst, pair_sem.at[2], pair_sem.at[3], sibling).wait_recv()
         diag_in.wait()
         for offset in range(ZN):
             across_landed(offset, 1)
 
         def columns(b):
-            sides = [jnp.concatenate([ag_ref[g * 8 + b * 4 + part] for part in range(4)], 0) for g in range(2)]
+            sides = [jnp.concatenate([ag_ref[part % 2 * 8 + g * 4 + b * 2 + part // 2] for part in range(4)], 0) for g in range(2)]
             for parity in range(2):
                 for g in range(2):
                     sides.append(
@@ -335,10 +361,10 @@
         for step in range(1, 9)
         for stream in STREAMS
     ]
-    plan += [(ADD_AT, add_up), (EXTRA_AT, begin_extra), (SOLVE_AT, solve_and_write)]
+    plan += [(SHARE_AT, share_blocks), (ADD_AT, add_up), (EXTRA_AT, begin_extra), (SOLVE_AT, solve_and_write)]
     plan += [
         (EXTRA_AT + EXTRA_STEP * (1 + (hops - 1) // REACH), functools.partial(x_landed, hops))
-        for hops in (4, 1, 2, 3, 8, 5, 6, 7)
+        for hops in (3, 1, 2, 6, 4, 5, 8, 7)
     ]
     for _, act in sorted(plan, key=lambda item: item[0]):
         act()
@@ -352,7 +378,8 @@
     for out in outs:
         out.wait()
     beta.wait_send()
-    for offset in range(1, RN):
+    share.wait_send()
+    for offset in range(1, 8):
         scatter(offset).wait_send()
         gather(offset).wait_send()
     for offset in range(ZN):
@@ -363,10 +390,25 @@
             for stream in STREAMS:
                 if runs(direction, step, stream):
                     hop(direction, step, stream).wait_send()
-    for hops in (0, REACH):
+    for hops in (0, REACH, 2 * REACH):
         for direction in range(2):
             for reach in x_far(direction, hops):
                 x_hop(direction, hops, reach).wait_send()
+
+
+def deliver(work_ref, gram_ref, work_out, gram_out, work_v, gram_v, sem_in, sem_out):
+    parts = work_ref.shape[0] // TILE
+    ways = [(work_ref, work_v, work_out, pl.ds(i * TILE, TILE)) for i in range(parts)]
+    ways.append((gram_ref, gram_v, gram_out, pl.ds(0, gram_ref.shape[0])))
+    ins = [pltpu.make_async_copy(a.at[rows], v.at[rows], sem_in.at[i]) for i, (a, v, _, rows) in enumerate(ways)]
+    outs = [pltpu.make_async_copy(v.at[rows], b.at[rows], sem_out.at[i]) for i, (_, v, b, rows) in enumerate(ways)]
+    for copy in ins:
+        copy.start()
+    for copy, out in zip(ins, outs):
+        copy.wait()
+        out.start()
+    for out in outs:
+        out.wait()
 
 
 def shards(rhs, panel_columns, diag_inverse, block_order):
@@ -378,7 +420,7 @@
     in_smem = pl.BlockSpec(memory_space=pltpu.SMEM)
     half = rows // 2
     span = width * 32 // RN
-    return pl.pallas_call(
+    work, gram = pl.pallas_call(
         whole,
         name="whole",
         out_shape=(
@@ -395,13 +437,14 @@
             pltpu.VMEM((2 * ZN, 80, 128), bf16),
             pltpu.VMEM((RN, 64, 128), bf16),
             pltpu.VMEM((RN, 80, 128), bf16),
-            pltpu.VMEM((RN, 80, 128), bf16),
+            pltpu.VMEM((8, 80, 128), bf16),
+            pltpu.VMEM((8, 80, 128), bf16),
             pltpu.VMEM((80, 128), bf16),
             pltpu.VMEM((2, BLOCK, width), bf16),
             pltpu.VMEM((2 * BLOCK, width), bf16),
             pltpu.VMEM((rows, width), bf16),
             pltpu.VMEM((span, width), jnp.float32),
-            dma((7,)), dma((RN,)), dma((RN,)), dma((RN,)), dma((RN,)), dma((2,)),
+            dma((7,)), dma((4,)), dma((8,)), dma((8,)), dma((8,)), dma((8,)), dma((2,)),
             dma((2, 9, 3)), dma((2, 9, 3)), dma((2,)), dma((ZN, 2)), dma((ZN, 2)),
             dma((2, 9)), dma((2, 9)), dma((2 * (half // TILE) + 1,)),
         ],
@@ -409,6 +452,23 @@
             collective_id=0, has_side_effects=True, vmem_limit_bytes=56 * 1024 * 1024
         ),
     )(block_order, diag_inverse, rhs, piece)
+    return pl.pallas_call(
+        deliver,
+        name="deliver",
+        out_shape=(
+            jax.ShapeDtypeStruct((rows, width), bf16),
+            jax.ShapeDtypeStruct((span, width), jnp.float32),
+        ),
+        in_specs=[any_space, any_space],
+        out_specs=(any_space, any_space),
+        scratch_shapes=[
+            pltpu.VMEM((rows, width), bf16),
+            pltpu.VMEM((span, width), jnp.float32),
+            dma((rows // TILE + 1,)),
+            dma((rows // TILE + 1,)),
+        ],
+        compiler_params=pltpu.CompilerParams(vmem_limit_bytes=60 * 1024 * 1024),
+    )(work, gram)
 
 
 def solution(mesh):

time: 66.3 us -> 62.4 us (0.941)
  local copies, waits for them, and re-layouts: 3.51 us -> 0 us
    unnamed x4 -> x0, local copies, waits for them, and re-layouts: 3.51 us -> none
    pallas_call x1, Pallas kernels: 62 us -> 59.1 us  [shards(): pl.pallas_call(whole, name='whole', out_shape=(jax.ShapeDtypeStruct((rows...]
    pallas_call x0 -> x1, Pallas kernels: none -> 2.43 us  [shards(): pl.pallas_call(deliver, name='deliver', out_shape=(jax.ShapeDtypeStruct((...]
where the time goes in v4:
time: 62.4 us; the launch traced here: 62.2 us
  Pallas kernels  61.6 us (99%)
  between operations  0.64 us (1%)
    pallas_call x1, Pallas kernels, shards(): pl.pallas_call(whole, name='whole', out_shape=(jax.ShapeDtypeStruct((rows...  59.1 us
    pallas_call x1, Pallas kernels, shards(): pl.pallas_call(deliver, name='deliver', out_shape=(jax.ShapeDtypeStruct((...  2.43 us

profile of v4, /device:TPU:6, one launch (start us, length us, event | category | flops | bytes accessed | tf_op | source)
XLA Modules:
  0.0 62.2 jit_solution(16015364028372274929)
XLA Ops:
  0.6 59.1 %whole.1 = (bf16[3072,256]{1,0:T(8,128)(2,1)}, f32[512,256]{1,0:T(8,128)}) custom-call(s32[192]{0:T(256)} %order_ref.1, f32[2,256,256]{2,1,0:T(8,128)} %diag_ref.1, bf16[3072,256]{1,0:T(8,128)(2,1)} %rhs_ref.1, bf16[16,3072]{1,0:T(8,128)(2,1)} %bitcast.1), custom_call_target="tpu_custom_call" | custom-call | tf_op jit(solution)/shard_map/whole/pallas_call | solution.py:423
  59.8 2.4 %deliver.1 = (bf16[3072,256]{1,0:T(8,128)(2,1)}, f32[512,256]{1,0:T(8,128)}) custom-call(bf16[3072,256]{1,0:T(8,128)(2,1)} %get-tuple-element.4.work_ref, f32[512,256]{1,0:T(8,128)} %get-tuple-element.5.gram_ref), custom_call_target="tpu_custom_call" | custom-call | tf_op jit(solution)/shard_map/deliver/pallas_call | solution.py:455

commit v5 on v4

--- a/solution.py
+++ b/solution.py
@@ -17,10 +17,10 @@
 FIRST = {NEAR: 3.5, FAR: 4.5, OTHER: 6.0}
 ADD_AT = 9.5
 EXTRA_AT = 17.0
-EXTRA_STEP = 4.5
+EXTRA_STEP = 4.4
 SHARE_AT = 18.0
-SOLVE_AT = 33.0
-REACH = 3
+SOLVE_AT = 37.0
+REACH = 2
 TILE = 512
 
 
@@ -174,7 +174,7 @@
                 remote(
                     dst, dst, x_send.at[direction, hops], x_recv.at[direction, hops], ring[direction]
                 ).wait_recv()
-                if hops in (REACH, 2 * REACH):
+                if hops in (2, 4, 6):
                     for reach in reversed(x_far(direction, hops)):
                         x_hop(direction, hops, reach).start()
                 across(origin(direction, hops), 1).start()
@@ -364,7 +364,7 @@
     plan += [(SHARE_AT, share_blocks), (ADD_AT, add_up), (EXTRA_AT, begin_extra), (SOLVE_AT, solve_and_write)]
     plan += [
         (EXTRA_AT + EXTRA_STEP * (1 + (hops - 1) // REACH), functools.partial(x_landed, hops))
-        for hops in (3, 1, 2, 6, 4, 5, 8, 7)
+        for hops in (2, 1, 4, 3, 6, 5, 8, 7)
     ]
     for _, act in sorted(plan, key=lambda item: item[0]):
         act()
@@ -390,7 +390,7 @@
             for stream in STREAMS:
                 if runs(direction, step, stream):
                     hop(direction, step, stream).wait_send()
-    for hops in (0, REACH, 2 * REACH):
+    for hops in (0, 2, 4, 6):
         for direction in range(2):
             for reach in x_far(direction, hops):
                 x_hop(direction, hops, reach).wait_send()

time: 62.4 us -> 63.6 us (1.019)
  Pallas kernels: 61.6 us -> 62.8 us
    pallas_call x1, Pallas kernels: 59.1 us -> 60.4 us  [shards(): pl.pallas_call(whole, name='whole', out_shape=(jax.ShapeDtypeStruct((rows...]
where the time goes in v5:
time: 63.6 us; the launch traced here: 63.4 us
  Pallas kernels  62.8 us (99%)
  between operations  0.64 us (1%)
    pallas_call x1, Pallas kernels, shards(): pl.pallas_call(whole, name='whole', out_shape=(jax.ShapeDtypeStruct((rows...  60.4 us
    pallas_call x1, Pallas kernels, shards(): pl.pallas_call(deliver, name='deliver', out_shape=(jax.ShapeDtypeStruct((...  2.43 us

profile of v5, /device:TPU:6, one launch (start us, length us, event | category | flops | bytes accessed | tf_op | source)
XLA Modules:
  0.0 63.4 jit_solution(10678859120512867396)
XLA Ops:
  0.6 60.4 %whole.1 = (bf16[3072,256]{1,0:T(8,128)(2,1)}, f32[512,256]{1,0:T(8,128)}) custom-call(s32[192]{0:T(256)} %order_ref.1, f32[2,256,256]{2,1,0:T(8,128)} %diag_ref.1, bf16[3072,256]{1,0:T(8,128)(2,1)} %rhs_ref.1, bf16[16,3072]{1,0:T(8,128)(2,1)} %bitcast.1), custom_call_target="tpu_custom_call" | custom-call | tf_op jit(solution)/shard_map/whole/pallas_call | solution.py:423
  61.0 2.4 %deliver.1 = (bf16[3072,256]{1,0:T(8,128)(2,1)}, f32[512,256]{1,0:T(8,128)}) custom-call(bf16[3072,256]{1,0:T(8,128)(2,1)} %get-tuple-element.4.work_ref, f32[512,256]{1,0:T(8,128)} %get-tuple-element.5.gram_ref), custom_call_target="tpu_custom_call" | custom-call | tf_op jit(solution)/shard_map/deliver/pallas_call | solution.py:455
